TPU v7x, 512 devices: a whole 4x8x8 slice. The times are simulated.
512 devices in a mesh: frame: 16 (over x, z_lo), height: 16 (over y, core), cand: 2 (over z_hi).
Axes of the slice: x: 4, y: 8, z: 8 (z_hi: 2, z_lo: 4; z = z_hi * 4 + z_lo), core: 2. Of those that a mesh axis runs over, the one named last changes fastest.
Arguments:
- queries: bfloat16 [64, 64, 16, 1536], P(('cand', 'frame'), 'height'), parts along dimension 0, may hold values from -6 to 6
- key_value: bfloat16 [2, 64, 64, 16, 1536], P(None, ('cand', 'frame'), 'height'), parts along dimension 1, may hold values from -6 to 6
- windows: int32 [12, 3], replicated, may hold values from 0 to 1, as said below
Outputs:
- attended: bfloat16 [64, 64, 16, 1536], P(('cand', 'frame'), 'height'), parts along dimension 0
There are 2 independent parts, one for each index of `cand`. A program takes and returns all parts, laid end to end along the dimension named above; an argument that names none is the same for every part. Nothing has to cross between parts.
Inputs may be any that keep to these rules, and one draw needn't show every extreme that they name: `windows`: column 0 is at most 1, column 1 at most 1, column 2 at most 1; each column reaches its most for some head and 0 for another.
All inputs are finite; a program needn't handle non-finite values.
Results may differ from a plain program's by a relative error of at most 0.0046.
Values may be sent and summed in bfloat16 or wider, within the bound.
A program may use at most 64 MiB of HBM per device.

v0:
```python
import functools
import math

import jax
import jax.numpy as jnp
from jax import lax
from jax.experimental import pallas as pl
from jax.experimental.pallas import tpu as pltpu
from jax.sharding import PartitionSpec as P

HEADS = 12
HALF = HEADS // 2
HD = 128
TOK = 128
CHIP = 2 * TOK
W = 16
TW = 8
NEG = -1e30
EXTRA = 16
SCALE = math.log2(math.e) / math.sqrt(HD)
MESH = pl.DeviceIdType.MESH


def dot(a, b, dims):
    return lax.dot_general(a, b, ((dims[0], dims[1]), ((), ())), preferred_element_type=jnp.float32)


PLANS = (
    (4, 2, 10),
    (4, 0, 8),
    (5, 2, 10),
    (6, 2, 10),
    (5, 0, 10),
    (7, 2, 12),
    (8, 2, 12),
    (7, 0, 12),
    (9, 2, 12),
    (12, 0, 12),
)


def sort_kernel(q, kv, win, packed, flags, choice, kvin, qin, order, sem):
    loads = (
        pltpu.make_async_copy(kv.at[0], kvin.at[0], sem.at[0]),
        pltpu.make_async_copy(kv.at[1], kvin.at[1], sem.at[1]),
        pltpu.make_async_copy(q, qin, sem.at[2]),
    )
    for load in loads:
        load.start()
    wf = [win[0, h] for h in range(HEADS)]
    wh = [win[1, h] for h in range(HEADS)]
    kinds = [(a - a * b, a * b, b - a * b, (1 - a) * (1 - b)) for a, b in zip(wf, wh)]
    count = [sum(kind[i] for kind in kinds) for i in range(4)]
    free = [jnp.int32(0), count[0], count[0] + count[1], count[0] + count[1] + count[2]]
    for h, kind in enumerate(kinds):
        rank = sum(x * place for x, place in zip(kind, free))
        free = [place + x for x, place in zip(kind, free)]
        order[rank] = jnp.int32(h)
        for i in range(3):
            flags[rank, i] = win[i, h]
        flags[h, 3] = rank
    wide, lone, tall = count[0] + count[1], count[0], count[1] + count[2]
    best = jnp.int32(len(PLANS) - 1)
    for i in reversed(range(len(PLANS) - 1)):
        nf, h0, h1 = PLANS[i]
        best = jnp.where((wide <= nf) & (lone >= h0) & (lone + tall <= h1), i, best)
    choice[0] = best
    for kind in range(3):
        loads[kind].wait()
        for s in range(HEADS):
            columns = pl.ds(pl.multiple_of(order[s] * HD, HD), HD)
            block = qin[:, columns] if kind == 2 else kvin[kind, :, columns]
            packed[s % 2, s // 2, kind] = block.T if kind == 1 else block


def place_kernel(o, flags, out):
    for h in range(HEADS):
        out[:, h * HD : (h + 1) * HD] = o[flags[h, 3]]


def kernel(
    cfg,
    n_frame,
    n_chip_y,
    packed,
    flags,
    out,
    kv,
    qa,
    acc,
    top,
    rs,
    rr,
    oh,
    own_l,
    own_s,
    own_r,
    z_s,
    z_r,
    q_s,
    q_r,
    ret_s,
    ret_r,
    o_l,
    o_s,
    o_r,
):
    nf, h0, h1 = cfg
    lo, hi = h0 // 2, h1 // 2
    halves = ((HALF // 2, HALF), (0, HALF // 2))
    runs = tuple((max(a, lo), min(b, hi)) for a, b in halves)
    f = lax.axis_index("frame")
    height = lax.axis_index("height")
    y = height // 2
    c = height % 2
    other = 1 - c
    z_ok = (f > 0, f < n_frame - 1)
    y_ok = (y > 0, y < n_chip_y - 1)
    z_dev = (f - 1, f + 1)
    y_dev = (y - 1, y + 1)
    partner = {"height": 2 * y + other}

    barrier = pltpu.get_barrier_semaphore()
    pl.semaphore_signal(barrier, inc=1, device_id=partner, device_id_type=MESH)
    for d in range(2):

        @pl.when(z_ok[d])
        def _():
            for g in range(2):
                pl.semaphore_signal(
                    barrier,
                    inc=1,
                    device_id={"frame": z_dev[d], "height": 2 * y + g},
                    device_id_type=MESH,
                )

        @pl.when(y_ok[d])
        def _():
            for g in range(2):
                pl.semaphore_signal(
                    barrier,
                    inc=1,
                    device_id={"height": 2 * y_dev[d] + g},
                    device_id_type=MESH,
                )

    def own_loads(i):
        j, n = halves[i][0], halves[i][1] - halves[i][0]
        return (
            pltpu.make_async_copy(
                packed.at[c, pl.ds(j, n), pl.ds(0, 2)], kv.at[1, pl.ds(j, n), c], own_l.at[i, 0]
            ),
            pltpu.make_async_copy(
                packed.at[c, pl.ds(j, n), 2], qa.at[pl.ds(j, n), 0, c], own_l.at[i, 1]
            ),
        )

    def remote(src, dst, send_sem, recv_sem, device):
        return pltpu.make_async_remote_copy(
            src_ref=src,
            dst_ref=dst,
            send_sem=send_sem,
            recv_sem=recv_sem,
            device_id=device,
            device_id_type=MESH,
        )

    def own_copies(i):
        j, n = halves[i][0], halves[i][1] - halves[i][0]
        return (
            remote(
                packed.at[other, pl.ds(j, n), pl.ds(0, 2)],
                kv.at[1, pl.ds(j, n), c],
                own_s.at[i, 0],
                own_r.at[i, 0],
                partner,
            ),
            remote(
                packed.at[other, pl.ds(j, n), 2],
                qa.at[pl.ds(j, n), 0, c],
                own_s.at[i, 1],
                own_r.at[i, 1],
                partner,
            ),
        )

    def z_copy(d, j, g):
        return remote(
            packed.at[g, j, pl.ds(0, 2)],
            kv.at[2 - 2 * d, j, c],
            z_s.at[d, j, g],
            z_r.at[1 - d, j, c],
            {"frame": z_dev[d], "height": 2 * y + g},
        )

    def z_arrival(d, j, half):
        dst = kv.at[2 * d, j, half]
        return remote(dst, dst, z_s.at[d, j, 0], z_r.at[d, j, half], partner)

    def q_copy(d, i, g):
        j, n = runs[i][0], runs[i][1] - runs[i][0]
        return remote(
            packed.at[g, pl.ds(j, n), 2],
            qa.at[pl.ds(j, n), 2 - d, c],
            q_s.at[d, i, g],
            q_r.at[1 - d, i, c],
            {"height": 2 * y_dev[d] + g},
        )

    def q_arrival(d, i, half):
        j, n = runs[i][0], runs[i][1] - runs[i][0]
        dst = qa.at[pl.ds(j, n), 1 + d, half]
        return remote(dst, dst, q_s.at[d, i, 0], q_r.at[d, i, half], partner)

    def ret_copy(d, j):
        return remote(
            rs.at[d, j],
            rr.at[1 - d, j],
            ret_s.at[d, j],
            ret_r.at[1 - d, j],
            {"height": 2 * y_dev[d] + c},
        )

    def o_copy(j):
        return remote(oh.at[j, other], out.at[2 * j + c], o_s.at[j], o_r.at[j], partner)

    def o_arrival(j):
        dst = out.at[2 * j + other]
        return remote(dst, dst, o_s.at[j], o_r.at[j], partner)

    def o_store(j):
        return pltpu.make_async_copy(oh.at[j, c], out.at[2 * j + c], o_l.at[j])

    for i in range(2):
        for copy in own_loads(i):
            copy.start()

    for d in range(2):

        @pl.when(jnp.logical_not(y_ok[d]))
        def _():
            rr[d] = jnp.zeros(rr.shape[1:], rr.dtype)

        @pl.when(jnp.logical_not(z_ok[d]))
        def _():
            kv[2 * d] = jnp.zeros(kv.shape[1:], kv.dtype)

    pl.semaphore_wait(
        barrier,
        1
        + 2 * sum(jnp.where(ok, 1, 0) for ok in z_ok)
        + 2 * sum(jnp.where(ok, 1, 0) for ok in y_ok),
    )

    def send_z(slots):
        for d in range(2):

            @pl.when(z_ok[d])
            def _():
                for s in slots:
                    z_copy(d, s // 2, s % 2).start()

    z_order = tuple(reversed(range(nf)))
    for copy in own_copies(0):
        copy.start()
    send_z(z_order[:4])
    for copy in own_copies(1):
        copy.start()
    for i in range(2):
        for d in range(2):

            @pl.when(y_ok[d])
            def _():
                for g in range(2):
                    q_copy(d, i, g).start()

    key_side = lax.broadcasted_iota(jnp.int32, (W, CHIP), 0) // TW
    query_side = lax.broadcasted_iota(jnp.int32, (W, CHIP), 1) % W // TW
    apart = jnp.where(key_side == query_side, 0.0, NEG).astype(jnp.float32)
    ones = jnp.ones((EXTRA, CHIP), jnp.bfloat16)

    def shut(j, column):
        return (1 - flags[2 * j + c, column]).astype(jnp.float32)

    def scores(tile, j, part, bias):
        k = kv[tile, j, :, 0].reshape(CHIP, HD)
        s = dot(k, qa[j, part].reshape(CHIP, HD), ((1,), (1,)))
        return (s.reshape(CHIP // W, W, CHIP) + bias[None]).reshape(CHIP, CHIP)

    def values(tile, j):
        vt = jnp.concatenate([kv[tile, j, 0, 1], kv[tile, j, 1, 1]], axis=1)
        return jnp.concatenate([vt, ones], axis=0)

    def weights(s, m):
        return jnp.exp2((s - m) * SCALE).astype(jnp.bfloat16)

    def here(j, parts):
        bias = apart * shut(j, 2)
        vt = values(1, j)
        found = [scores(1, j, part, bias) for part in parts]
        tops = [jnp.max(s, axis=0, keepdims=True) for s in found]
        sums = [dot(vt, weights(s, m), ((1,), (0,))) for s, m in zip(found, tops)]
        for part, m, o in zip(parts, tops, sums):
            top[j, part, 0:1] = m
            acc[j, part] = o

    def around(j, parts):
        width = apart * shut(j, 2)
        closed = shut(j, 0) * NEG
        bias = [width + jnp.where(z_ok[d], closed, NEG) for d in range(2)]
        bias = jnp.stack(bias)[:, None]
        vt = jnp.concatenate([values(0, j), values(2, j)], axis=1)
        k = jnp.concatenate([kv[2 * d, j, :, 0].reshape(CHIP, HD) for d in range(2)], axis=0)
        found = []
        for part in parts:
            s = dot(k, qa[j, part].reshape(CHIP, HD), ((1,), (1,)))
            found.append((s.reshape(2, CHIP // W, W, CHIP) + bias).reshape(2 * CHIP, CHIP))
        old = [top[j, part, 0:1] for part in parts]
        before = [acc[j, part] for part in parts]
        results = []
        for s, m_old, o_old in zip(found, old, before):
            m = jnp.maximum(m_old, jnp.max(s, axis=0, keepdims=True))
            o = o_old * jnp.exp2((m_old - m) * SCALE) + dot(vt, weights(s, m), ((1,), (0,)))
            results.append((m, o))
        for part, (m, o) in zip(parts, results):
            top[j, part, 0:1] = m
            acc[j, part] = o

    def give_back(j):
        for d in range(2):
            m = top[j, d + 1, 0:1]
            total = acc[j, d + 1, HD : HD + 1]
            rs[d, j, 0:HD] = (acc[j, d + 1, 0:HD] * (1.0 / total)).astype(jnp.bfloat16)
            level = m * SCALE + jnp.log2(total)
            a = level.astype(jnp.bfloat16).astype(jnp.float32)
            b = (level - a).astype(jnp.bfloat16).astype(jnp.float32)
            row = lax.broadcasted_iota(jnp.int32, (EXTRA, CHIP), 0)
            rest = jnp.where(row == 2, level - a - b, 0.0)
            digits = jnp.where(row == 0, a, jnp.where(row == 1, b, rest))
            rs[d, j, HD : HD + EXTRA] = digits.astype(jnp.bfloat16)
        for d in range(2):

            @pl.when(y_ok[d])
            def _():
                ret_copy(d, j).start()

    def finish(j, o):
        o = o.T.astype(jnp.bfloat16)
        oh[j, 0] = o[:TOK]
        oh[j, 1] = o[TOK:]
        o_copy(j).start()
        o_store(j).start()

    def alone(j):
        finish(j, acc[j, 0, 0:HD] * (1.0 / acc[j, 0, HD : HD + 1]))

    def join(j):
        for d in range(2):

            @pl.when(y_ok[d])
            def _():
                ret_copy(1 - d, j).wait_recv()

        m = top[j, 0, 0:1] * SCALE
        total = acc[j, 0, HD : HD + 1]
        low = shut(j, 1) * NEG
        levels = []
        for d in range(2):
            level = jnp.sum(rr[d, j, HD : HD + EXTRA].astype(jnp.float32), axis=0, keepdims=True)
            levels.append(level + jnp.where(y_ok[d], low, NEG))
        best = jnp.maximum(m + jnp.log2(total), jnp.maximum(levels[0], levels[1]))
        w = [jnp.exp2(x - best) for x in (m, *levels)]
        over = 1.0 / (total * w[0] + w[1] + w[2])
        o = acc[j, 0, 0:HD] * (w[0] * over)
        for d in range(2):
            o = o + rr[d, j, 0:HD].astype(jnp.float32) * (w[d + 1] * over)
        finish(j, o)

    my_z = (nf + 1 - c) // 2
    both = (0, 1, 2)

    for i in range(2):
        for copy in own_loads(i):
            copy.wait()
        for copy in own_copies(i):
            copy.wait_recv()
        first, last = runs[i]
        for a, b in ((halves[i][0], first), (last, halves[i][1])):
            for j in range(a, b):
                here(j, (0,))

    send_z(z_order[4:])

    for i in range(2):
        first, last = runs[i]
        for d in range(2):

            @pl.when(y_ok[d])
            def _():
                for half in range(2):
                    q_arrival(d, i, half).wait_recv()

        @pl.loop(0, last - first)
        def _(n):
            j = last - 1 - n
            here(j, both)

            @pl.when(j >= my_z)
            def _():
                give_back(j)

    @pl.loop(jnp.maximum(my_z, hi), HALF)
    def _(j):
        alone(j)

    @pl.loop(0, hi - jnp.maximum(my_z, lo))
    def _(n):
        join(hi - 1 - n)

    for i in range(2):
        for copy in own_copies(i):
            copy.wait_send()
    for d in range(2):

        @pl.when(y_ok[d])
        def _():
            for i in range(2):
                for g in range(2):
                    q_copy(d, i, g).wait_send()

    def wait_z(j):
        for d in range(2):

            @pl.when(z_ok[d])
            def _():
                for half in range(2):
                    z_arrival(d, j, half).wait_recv()

    @pl.loop(0, my_z - lo)
    def _(n):
        j = my_z - 1 - n
        wait_z(j)
        around(j, both)
        give_back(j)

    for j in reversed(range(lo)):
        wait_z(j)
        around(j, (0,))
        alone(j)

    @pl.loop(0, my_z - lo)
    def _(n):
        join(my_z - 1 - n)

    for d in range(2):

        @pl.when(z_ok[d])
        def _():
            for s in range(nf):
                z_copy(d, s // 2, s % 2).wait_send()

        @pl.when(y_ok[d])
        def _():
            @pl.loop(lo, hi)
            def _(j):
                ret_copy(d, j).wait_send()

    @pl.loop(0, HALF)
    def _(j):
        o_store(j).wait()
        o_copy(j).wait_send()
        o_arrival(j).wait_recv()


def attend(index, n_frame, n_chip_y, packed, flags):
    nf, h0, h1 = PLANS[index]
    assert h0 % 2 == 0 and h1 % 2 == 0 and h0 <= min(nf, HALF - 2) and max(nf, HALF + 2) <= h1
    bf16, f32 = jnp.bfloat16, jnp.float32
    dma = pltpu.SemaphoreType.DMA
    return pl.pallas_call(
        functools.partial(kernel, PLANS[index], n_frame, n_chip_y),
        out_shape=jax.ShapeDtypeStruct((HEADS, TOK, HD), bf16),
        in_specs=[pl.BlockSpec(memory_space=pl.ANY), pl.BlockSpec(memory_space=pltpu.SMEM)],
        out_specs=pl.BlockSpec(memory_space=pl.ANY),
        scratch_shapes=[
            pltpu.VMEM((3, HALF, 2, 2, TOK, HD), bf16),
            pltpu.VMEM((HALF, 3, 2, TOK, HD), bf16),
            pltpu.VMEM((HALF, 3, HD + EXTRA, CHIP), f32),
            pltpu.VMEM((HALF, 3, 8, CHIP), f32),
            pltpu.VMEM((2, HALF, HD + EXTRA, CHIP), bf16),
            pltpu.VMEM((2, HALF, HD + EXTRA, CHIP), bf16),
            pltpu.VMEM((HALF, 2, TOK, HD), bf16),
            dma((2, 2)),
            dma((2, 2)),
            dma((2, 2)),
            dma((2, HALF, 2)),
            dma((2, HALF, 2)),
            dma((2, 2, 2)),
            dma((2, 2, 2)),
            dma((2, HALF)),
            dma((2, HALF)),
            dma((HALF,)),
            dma((HALF,)),
            dma((HALF,)),
        ],
        compiler_params=pltpu.CompilerParams(
            collective_id=index,
            has_side_effects=True,
            vmem_limit_bytes=32 * 1024 * 1024,
        ),
    )(packed, flags)


def shards(queries, key_value, windows):
    n_frame = lax.axis_size("frame")
    n_chip_y = lax.axis_size("height") // 2
    width = HEADS * HD
    vmem = pl.BlockSpec(memory_space=pltpu.VMEM)
    smem = pl.BlockSpec(memory_space=pltpu.SMEM)
    packed, flags, choice = pl.pallas_call(
        sort_kernel,
        out_shape=(
            jax.ShapeDtypeStruct((2, HALF, 3, TOK, HD), jnp.bfloat16),
            jax.ShapeDtypeStruct((HEADS, 4), jnp.int32),
            jax.ShapeDtypeStruct((1,), jnp.int32),
        ),
        in_specs=[pl.BlockSpec(memory_space=pl.ANY), pl.BlockSpec(memory_space=pl.ANY), smem],
        out_specs=(vmem, smem, smem),
        scratch_shapes=[
            pltpu.VMEM((2, TOK, width), jnp.bfloat16),
            pltpu.VMEM((TOK, width), jnp.bfloat16),
            pltpu.SMEM((HEADS,), jnp.int32),
            pltpu.SemaphoreType.DMA((3,)),
        ],
    )(queries.reshape(TOK, width), key_value.reshape(2, TOK, width), windows.T)
    branches = [functools.partial(attend, i, n_frame, n_chip_y) for i in range(len(PLANS))]
    slots = lax.switch(choice[0], branches, packed, flags)
    result = pl.pallas_call(
        place_kernel,
        out_shape=jax.ShapeDtypeStruct((TOK, width), jnp.bfloat16),
        in_specs=[vmem, smem],
        out_specs=vmem,
    )(slots, flags)
    return result.reshape(queries.shape)


def solution(mesh):
    in_specs = (
        P(("cand", "frame"), "height", None, None),
        P(None, ("cand", "frame"), "height", None, None),
        P(),
    )
    out_specs = P(("cand", "frame"), "height", None, None)
    return jax.shard_map(shards, mesh=mesh, in_specs=in_specs, out_specs=out_specs, check_vma=False)
```

profile of v0, /device:TPU:23, one launch (start us, length us, event | category | flops | bytes accessed | tf_op | source)
XLA Modules:
  0.0 35.0 jit_solution(2168541108414231318)
XLA Ops:
  0.0 2.8 %shard_map.37 = (bf16[2,6,3,128,128]{4,3,2,1,0:T(8,128)(2,1)S(1)}, s32[12,4]{1,0:T(8,128)S(1)}, s32[1]{0:T(128)}) custom-call(bf16[128,1536]{1,0:T(8,128)(2,1)} %bitcast.6, bf16[2,128,1536]{2,1,0:T(8,128)(2,1)} %bitcast.5, s32[3,12]{1,0:T(4,128)} %bitcast.7), custom_call_target="tpu_custom_call" | custom-call | tf_op jit(solution)/shard_map/pallas_call | solution.py:520
  3.4 30.0 %conditional.1 = (bf16[12,128,128]{2,1,0:T(8,128)(2,1)S(1)}) conditional(s32[]{:T(128)} %bitcast.3, (bf16[2,6,3,128,128]{4,3,2,1,0:T(8,128)(2,1)S(1)}, s32[12,4]{1,0:T(8,128)S(1)}) %tuple.35, (bf16[2,6,3,128,128]{4,3,2,1,0:T(8,128)(2,1)S(1)}, s32[12,4]{1,0:T(8,128)S(1)}) %tuple.35, ...), branch_computations={%region_0.0_spmd, %region_1.0_spmd, %region_2.0_spmd, %region_3.0_... | conditional | bytes 8 | solution.py:537
  3.5 29.4 %branch_2_fun.1 = bf16[12,128,128]{2,1,0:T(8,128)(2,1)S(1)} custom-call(bf16[2,6,3,128,128]{4,3,2,1,0:T(8,128)(2,1)S(1)} %get-tuple-element.55.packed, s32[12,4]{1,0:T(8,128)S(1)} %get-tuple-element.56.flags), custom_call_target="tpu_custom_call" | custom-call | tf_op jit(solution)/shard_map/cond/branch_2_fun/pallas_call | solution.py:480
  33.5 1.5 %shard_map.38 = bf16[128,1536]{1,0:T(8,128)(2,1)} custom-call(bf16[12,128,128]{2,1,0:T(8,128)(2,1)S(1)} %get-tuple-element.82.o, s32[12,4]{1,0:T(8,128)S(1)} %get-tuple-element.81.flags), custom_call_target="tpu_custom_call" | custom-call | tf_op jit(solution)/shard_map/pallas_call | solution.py:538
where the time goes:
time: 35.1 us; the launch traced here: 35 us
  Pallas kernels  33.7 us (96%)
  between operations  0.67 us (2%)
  loops' own time  0.65 us (2%)
    pallas_call x1, Pallas kernels, attend(): pl.pallas_call(functools.partial(kernel, PLANS[index], n_frame, n_chip_y)...  29.4 us
    pallas_call x1, Pallas kernels, shards(): pl.pallas_call(sort_kernel, out_shape=(jax.ShapeDtypeStruct((2, HALF, 3,...  2.78 us
    pallas_call x1, Pallas kernels, shards(): pl.pallas_call(place_kernel, out_shape=jax.ShapeDtypeStruct((TOK, width),...  1.49 us

commit v1 on v0

v1 whole, which is shorter than its diff:
```python
import functools
import math

import jax
import jax.numpy as jnp
from jax import lax
from jax.experimental import pallas as pl
from jax.experimental.pallas import tpu as pltpu
from jax.sharding import PartitionSpec as P

HEADS = 12
HALF = HEADS // 2
HD = 128
TOK = 128
CHIP = 2 * TOK
W = 16
TW = 8
NEG = -1e30
EXTRA = 16
SCALE = math.log2(math.e) / math.sqrt(HD)
MESH = pl.DeviceIdType.MESH


def dot(a, b, dims):
    return lax.dot_general(a, b, ((dims[0], dims[1]), ((), ())), preferred_element_type=jnp.float32)


PLANS = (
    (4, 2, 10),
    (4, 0, 8),
    (5, 2, 10),
    (6, 2, 10),
    (5, 0, 10),
    (7, 2, 12),
    (8, 2, 12),
    (7, 0, 12),
    (9, 2, 12),
    (12, 0, 12),
)


def sort_kernel(q, kv, win, packed, flags, choice):
    wf = [win[0, h] for h in range(HEADS)]
    wh = [win[1, h] for h in range(HEADS)]
    kinds = [(a - a * b, a * b, b - a * b, (1 - a) * (1 - b)) for a, b in zip(wf, wh)]
    count = [sum(kind[i] for kind in kinds) for i in range(4)]
    free = [jnp.int32(0), count[0], count[0] + count[1], count[0] + count[1] + count[2]]
    ranks = []
    for kind in kinds:
        ranks.append(sum(x * place for x, place in zip(kind, free)))
        free = [place + x for x, place in zip(kind, free)]
    heads = [sum(jnp.where(ranks[h] == s, h, 0) for h in range(HEADS)) for s in range(HEADS)]
    wide, lone, tall = count[0] + count[1], count[0], count[1] + count[2]
    best = jnp.int32(len(PLANS) - 1)
    for i in reversed(range(len(PLANS) - 1)):
        nf, h0, h1 = PLANS[i]
        best = jnp.where((wide <= nf) & (lone >= h0) & (lone + tall <= h1), i, best)
    choice[0] = best
    for s in range(HEADS):
        for i in range(3):
            flags[s, i] = win[i, heads[s]]
        flags[s, 3] = ranks[s]
        columns = pl.ds(pl.multiple_of(heads[s] * HD, HD), HD)
        packed[s % 2, s // 2, 0] = kv[0, :, columns]
        packed[s % 2, s // 2, 1] = kv[1, :, columns].T
        packed[s % 2, s // 2, 2] = q[:, columns]


def place_kernel(o, flags, out):
    for h in range(HEADS):
        out[:, h * HD : (h + 1) * HD] = o[flags[h, 3]]


def kernel(
    cfg,
    n_frame,
    n_chip_y,
    packed,
    flags,
    out,
    kv,
    qa,
    acc,
    top,
    rs,
    rr,
    oh,
    own_l,
    own_s,
    own_r,
    z_s,
    z_r,
    q_s,
    q_r,
    ret_s,
    ret_r,
    o_l,
    o_s,
    o_r,
):
    nf, h0, h1 = cfg
    lo, hi = h0 // 2, h1 // 2
    f = lax.axis_index("frame")
    height = lax.axis_index("height")
    y = height // 2
    c = height % 2
    other = 1 - c
    z_ok = (f > 0, f < n_frame - 1)
    y_ok = (y > 0, y < n_chip_y - 1)
    z_dev = (f - 1, f + 1)
    y_dev = (y - 1, y + 1)
    partner = {"height": 2 * y + other}

    barrier = pltpu.get_barrier_semaphore()
    pl.semaphore_signal(barrier, inc=1, device_id=partner, device_id_type=MESH)
    for d in range(2):

        @pl.when(z_ok[d])
        def _():
            for g in range(2):
                pl.semaphore_signal(
                    barrier,
                    inc=1,
                    device_id={"frame": z_dev[d], "height": 2 * y + g},
                    device_id_type=MESH,
                )

        @pl.when(y_ok[d])
        def _():
            for g in range(2):
                pl.semaphore_signal(
                    barrier,
                    inc=1,
                    device_id={"height": 2 * y_dev[d] + g},
                    device_id_type=MESH,
                )

    own_loads = (
        pltpu.make_async_copy(packed.at[c, :, pl.ds(0, 2)], kv.at[1, :, c], own_l.at[0]),
        pltpu.make_async_copy(packed.at[c, :, 2], qa.at[:, 0, c], own_l.at[1]),
    )

    def remote(src, dst, send_sem, recv_sem, device):
        return pltpu.make_async_remote_copy(
            src_ref=src,
            dst_ref=dst,
            send_sem=send_sem,
            recv_sem=recv_sem,
            device_id=device,
            device_id_type=MESH,
        )

    own_copies = (
        remote(
            packed.at[other, :, pl.ds(0, 2)], kv.at[1, :, c], own_s.at[0], own_r.at[0], partner
        ),
        remote(packed.at[other, :, 2], qa.at[:, 0, c], own_s.at[1], own_r.at[1], partner),
    )

    def z_copy(d, j, g):
        return remote(
            packed.at[g, j, pl.ds(0, 2)],
            kv.at[2 - 2 * d, j, c],
            z_s.at[d, j, g],
            z_r.at[1 - d, j, c],
            {"frame": z_dev[d], "height": 2 * y + g},
        )

    def z_arrival(d, j, half):
        dst = kv.at[2 * d, j, half]
        return remote(dst, dst, z_s.at[d, j, 0], z_r.at[d, j, half], partner)

    def q_copy(d, j, g):
        return remote(
            packed.at[g, j, 2],
            qa.at[j, 2 - d, c],
            q_s.at[d, j, g],
            q_r.at[1 - d, j, c],
            {"height": 2 * y_dev[d] + g},
        )

    def q_arrival(d, j, half):
        dst = qa.at[j, 1 + d, half]
        return remote(dst, dst, q_s.at[d, j, 0], q_r.at[d, j, half], partner)

    def ret_copy(d, j):
        return remote(
            rs.at[d, j],
            rr.at[1 - d, j],
            ret_s.at[d, j],
            ret_r.at[1 - d, j],
            {"height": 2 * y_dev[d] + c},
        )

    def o_copy(j):
        return remote(oh.at[j, other], out.at[2 * j + c], o_s.at[j], o_r.at[j], partner)

    def o_arrival(j):
        dst = out.at[2 * j + other]
        return remote(dst, dst, o_s.at[j], o_r.at[j], partner)

    def o_store(j):
        return pltpu.make_async_copy(oh.at[j, c], out.at[2 * j + c], o_l.at[j])

    for copy in own_loads:
        copy.start()

    for d in range(2):

        @pl.when(jnp.logical_not(y_ok[d]))
        def _():
            rr[d] = jnp.zeros(rr.shape[1:], rr.dtype)

        @pl.when(jnp.logical_not(z_ok[d]))
        def _():
            kv[2 * d] = jnp.zeros(kv.shape[1:], kv.dtype)

    pl.semaphore_wait(
        barrier,
        1
        + 2 * sum(jnp.where(ok, 1, 0) for ok in z_ok)
        + 2 * sum(jnp.where(ok, 1, 0) for ok in y_ok),
    )

    def send_z(slots):
        for d in range(2):

            @pl.when(z_ok[d])
            def _():
                for s in slots:
                    z_copy(d, s // 2, s % 2).start()

    z_order = tuple(reversed(range(nf)))
    for copy in own_copies:
        copy.start()
    send_z(z_order[:4])
    few, most = nf // 2, (nf + 1) // 2

    @pl.loop(lo, hi)
    def _(n):
        j = jnp.where(n < most, most - 1 - n + lo, n)
        for d in range(2):

            @pl.when(y_ok[d])
            def _():
                for g in range(2):
                    q_copy(d, j, g).start()

    key_side = lax.broadcasted_iota(jnp.int32, (W, 3 * CHIP), 0) // TW
    query_side = lax.broadcasted_iota(jnp.int32, (W, 3 * CHIP), 1) % W // TW
    apart = jnp.where(key_side == query_side, 0.0, NEG).astype(jnp.float32)
    ones = jnp.ones((EXTRA, CHIP), jnp.bfloat16)

    def shut(j, column):
        return (1 - flags[2 * j + c, column]).astype(jnp.float32)

    def keys(tile, j):
        return kv[tile, j, :, 0].reshape(CHIP, HD)

    def values(tile, j):
        vt = jnp.concatenate([kv[tile, j, 0, 1], kv[tile, j, 1, 1]], axis=1)
        return jnp.concatenate([vt, ones], axis=0)

    def scores(k, j, parts):
        q = qa[j, 0:parts].reshape(parts * CHIP, HD)
        return dot(k, q, ((1,), (1,)))

    def weights(s, m):
        return jnp.exp2((s - m) * SCALE).astype(jnp.bfloat16)

    def here(j, parts):
        n = parts * CHIP
        s = scores(keys(1, j), j, parts)
        bias = apart[:, :n] * shut(j, 2)
        s = (s.reshape(CHIP // W, W, n) + bias[None]).reshape(CHIP, n)
        m = jnp.max(s, axis=0, keepdims=True)
        top[j, 0:1, 0:n] = m
        acc[j, :, 0:n] = dot(values(1, j), weights(s, m), ((1,), (0,)))

    def around(j, parts):
        for d in range(2):

            @pl.when(z_ok[d])
            def _():
                for half in range(2):
                    z_arrival(d, j, half).wait_recv()

        n = parts * CHIP
        s = scores(jnp.concatenate([keys(0, j), keys(2, j)], axis=0), j, parts)
        width = apart[:, :n] * shut(j, 2)
        closed = shut(j, 0) * NEG
        bias = jnp.stack([width + jnp.where(z_ok[d], closed, NEG) for d in range(2)])[:, None]
        s = (s.reshape(2, CHIP // W, W, n) + bias).reshape(2 * CHIP, n)
        m_old = top[j, 0:1, 0:n]
        m = jnp.maximum(m_old, jnp.max(s, axis=0, keepdims=True))
        vt = jnp.concatenate([values(0, j), values(2, j)], axis=1)
        fade = jnp.exp2((m_old - m) * SCALE)
        top[j, 0:1, 0:n] = m
        acc[j, :, 0:n] = acc[j, :, 0:n] * fade + dot(vt, weights(s, m), ((1,), (0,)))

    def give_back(j):
        n = slice(CHIP, 3 * CHIP)
        m = top[j, 0:1, n]
        total = acc[j, HD : HD + 1, n]
        o = (acc[j, 0:HD, n] * (1.0 / total)).astype(jnp.bfloat16)
        level = m * SCALE + jnp.log2(total)
        a = level.astype(jnp.bfloat16).astype(jnp.float32)
        b = (level - a).astype(jnp.bfloat16).astype(jnp.float32)
        row = lax.broadcasted_iota(jnp.int32, (EXTRA, 2 * CHIP), 0)
        rest = jnp.where(row == 2, level - a - b, 0.0)
        digits = jnp.where(row == 0, a, jnp.where(row == 1, b, rest)).astype(jnp.bfloat16)
        for d in range(2):
            rs[d, j, 0:HD] = o[:, d * CHIP : (d + 1) * CHIP]
            rs[d, j, HD : HD + EXTRA] = digits[:, d * CHIP : (d + 1) * CHIP]
        for d in range(2):

            @pl.when(y_ok[d])
            def _():
                ret_copy(d, j).start()

    def finish(j, o):
        o = o.T.astype(jnp.bfloat16)
        oh[j, 0] = o[:TOK]
        oh[j, 1] = o[TOK:]
        o_copy(j).start()
        o_store(j).start()

    def alone(j):
        finish(j, acc[j, 0:HD, 0:CHIP] * (1.0 / acc[j, HD : HD + 1, 0:CHIP]))

    def join(j):
        for d in range(2):

            @pl.when(y_ok[d])
            def _():
                ret_copy(1 - d, j).wait_recv()

        m = top[j, 0:1, 0:CHIP] * SCALE
        total = acc[j, HD : HD + 1, 0:CHIP]
        low = shut(j, 1) * NEG
        levels = []
        for d in range(2):
            digits = rr[d, j, HD : HD + EXTRA].astype(jnp.float32)
            level = jnp.sum(digits, axis=0, keepdims=True)
            levels.append(level + jnp.where(y_ok[d], low, NEG))
        best = jnp.maximum(m + jnp.log2(total), jnp.maximum(levels[0], levels[1]))
        w = [jnp.exp2(x - best) for x in (m, *levels)]
        over = 1.0 / (total * w[0] + w[1] + w[2])
        o = acc[j, 0:HD, 0:CHIP] * (w[0] * over)
        for d in range(2):
            o = o + rr[d, j, 0:HD].astype(jnp.float32) * (w[d + 1] * over)
        finish(j, o)

    for copy in own_loads:
        copy.wait()
    for copy in own_copies:
        copy.wait_recv()

    if lo + HALF - hi > 0:

        @pl.loop(0, lo + HALF - hi)
        def _(n):
            j = jnp.where(n < lo, n, n - lo + hi)
            here(j, 1)

            @pl.when(j >= hi)
            def _():
                alone(j)

    send_z(z_order[4:])

    my_z = (nf + 1 - c) // 2
    n_in = my_z - lo
    n_out = hi - my_z

    @pl.loop(0, 2 * n_in + n_out)
    def _(n):
        outer = (n == n_in) | (n > n_in + n_out)
        j_in = jnp.where(n < n_in, my_z - 1 - n, my_z - 1 + n - n_in)
        j_out = jnp.where(n == n_in, my_z - 1, my_z - 1 - (n - n_in - n_out))
        j = jnp.where(outer, j_out, j_in)

        @pl.when(jnp.logical_not(outer))
        def _():
            for d in range(2):

                @pl.when(y_ok[d])
                def _():
                    for half in range(2):
                        q_arrival(d, j, half).wait_recv()

            here(j, 3)

        @pl.when(outer)
        def _():
            around(j, 3)

        @pl.when(n >= n_in)
        def _():
            give_back(j)

    for copy in own_copies:
        copy.wait_send()

    if lo > 0:

        @pl.loop(0, lo)
        def _(j):
            around(j, 1)
            alone(j)

    @pl.loop(0, hi - lo)
    def _(n):
        join(jnp.where(n < n_out, my_z + n, my_z - 1 - (n - n_out)))

    for d in range(2):

        @pl.when(z_ok[d])
        def _():
            for s in range(nf):
                z_copy(d, s // 2, s % 2).wait_send()

        @pl.when(y_ok[d])
        def _():
            @pl.loop(lo, hi)
            def _(j):
                for g in range(2):
                    q_copy(d, j, g).wait_send()
                ret_copy(d, j).wait_send()

    @pl.loop(0, HALF)
    def _(j):
        o_store(j).wait()
        o_copy(j).wait_send()
        o_arrival(j).wait_recv()


def attend(index, n_frame, n_chip_y, packed, flags):
    nf, h0, h1 = PLANS[index]
    assert h0 % 2 == 0 and h1 % 2 == 0 and h0 < nf - 1 and nf <= h1
    bf16, f32 = jnp.bfloat16, jnp.float32
    dma = pltpu.SemaphoreType.DMA
    return pl.pallas_call(
        functools.partial(kernel, PLANS[index], n_frame, n_chip_y),
        out_shape=jax.ShapeDtypeStruct((HEADS, TOK, HD), bf16),
        in_specs=[pl.BlockSpec(memory_space=pl.ANY), pl.BlockSpec(memory_space=pltpu.SMEM)],
        out_specs=pl.BlockSpec(memory_space=pl.ANY),
        scratch_shapes=[
            pltpu.VMEM((3, HALF, 2, 2, TOK, HD), bf16),
            pltpu.VMEM((HALF, 3, 2, TOK, HD), bf16),
            pltpu.VMEM((HALF, HD + EXTRA, 3 * CHIP), f32),
            pltpu.VMEM((HALF, 8, 3 * CHIP), f32),
            pltpu.VMEM((2, HALF, HD + EXTRA, CHIP), bf16),
            pltpu.VMEM((2, HALF, HD + EXTRA, CHIP), bf16),
            pltpu.VMEM((HALF, 2, TOK, HD), bf16),
            dma((2,)),
            dma((2,)),
            dma((2,)),
            dma((2, HALF, 2)),
            dma((2, HALF, 2)),
            dma((2, HALF, 2)),
            dma((2, HALF, 2)),
            dma((2, HALF)),
            dma((2, HALF)),
            dma((HALF,)),
            dma((HALF,)),
            dma((HALF,)),
        ],
        compiler_params=pltpu.CompilerParams(
            collective_id=index,
            has_side_effects=True,
            vmem_limit_bytes=32 * 1024 * 1024,
        ),
    )(packed, flags)


def shards(queries, key_value, windows):
    n_frame = lax.axis_size("frame")
    n_chip_y = lax.axis_size("height") // 2
    width = HEADS * HD
    vmem = pl.BlockSpec(memory_space=pltpu.VMEM)
    smem = pl.BlockSpec(memory_space=pltpu.SMEM)
    packed, flags, choice = pl.pallas_call(
        sort_kernel,
        out_shape=(
            jax.ShapeDtypeStruct((2, HALF, 3, TOK, HD), jnp.bfloat16),
            jax.ShapeDtypeStruct((HEADS, 4), jnp.int32),
            jax.ShapeDtypeStruct((1,), jnp.int32),
        ),
        in_specs=[vmem, vmem, smem],
        out_specs=(vmem, smem, smem),
    )(queries.reshape(TOK, width), key_value.reshape(2, TOK, width), windows.T)
    branches = [functools.partial(attend, i, n_frame, n_chip_y) for i in range(len(PLANS))]
    slots = lax.switch(choice[0], branches, packed, flags)
    result = pl.pallas_call(
        place_kernel,
        out_shape=jax.ShapeDtypeStruct((TOK, width), jnp.bfloat16),
        in_specs=[vmem, smem],
        out_specs=vmem,
    )(slots, flags)
    return result.reshape(queries.shape)


def solution(mesh):
    in_specs = (
        P(("cand", "frame"), "height", None, None),
        P(None, ("cand", "frame"), "height", None, None),
        P(),
    )
    out_specs = P(("cand", "frame"), "height", None, None)
    return jax.shard_map(shards, mesh=mesh, in_specs=in_specs, out_specs=out_specs, check_vma=False)
```

time: 35.1 us -> 37.4 us (1.066)
  the two profiles are of different devices: /device:TPU:23 before, /device:TPU:31 now
where the time goes in v1:
time: 37.4 us; the launch traced here: 37.3 us
  Pallas kernels  36.3 us (97%)
  between operations  0.67 us (2%)
    pallas_call x1, Pallas kernels, attend(): pl.pallas_call(functools.partial(kernel, PLANS[index], n_frame, n_chip_y)...  32.4 us
    pallas_call x1, Pallas kernels, shards(): pl.pallas_call(sort_kernel, out_shape=(jax.ShapeDtypeStruct((2, HALF, 3,...  2.42 us
    pallas_call x1, Pallas kernels, shards(): pl.pallas_call(place_kernel, out_shape=jax.ShapeDtypeStruct((TOK, width),...  1.49 us

profile of v1, /device:TPU:31, one launch (start us, length us, event | category | flops | bytes accessed | tf_op | source)
XLA Modules:
  0.0 37.3 jit_solution(2332140866061303600)
XLA Ops:
  0.0 2.4 %shard_map.37 = (bf16[2,6,3,128,128]{4,3,2,1,0:T(8,128)(2,1)S(1)}, s32[12,4]{1,0:T(8,128)S(1)}, s32[1]{0:T(128)}) custom-call(bf16[128,1536]{1,0:T(8,128)(2,1)} %bitcast.6, bf16[2,128,1536]{2,1,0:T(8,128)(2,1)} %bitcast.5, s32[3,12]{1,0:T(4,128)} %bitcast.7), custom_call_target="tpu_custom_call" | custom-call | tf_op jit(solution)/shard_map/pallas_call | solution.py:483
  3.1 32.7 %conditional.1 = (bf16[12,128,128]{2,1,0:T(8,128)(2,1)S(1)}) conditional(s32[]{:T(128)} %bitcast.3, (bf16[2,6,3,128,128]{4,3,2,1,0:T(8,128)(2,1)S(1)}, s32[12,4]{1,0:T(8,128)S(1)}) %tuple.35, (bf16[2,6,3,128,128]{4,3,2,1,0:T(8,128)(2,1)S(1)}, s32[12,4]{1,0:T(8,128)S(1)}) %tuple.35, ...), branch_computations={%region_0.0_spmd, %region_1.0_spmd, %region_2.0_spmd, %region_3.0_... | conditional | bytes 8 | solution.py:494
  3.1 32.4 %branch_3_fun.1 = bf16[12,128,128]{2,1,0:T(8,128)(2,1)S(1)} custom-call(bf16[2,6,3,128,128]{4,3,2,1,0:T(8,128)(2,1)S(1)} %get-tuple-element.60.packed, s32[12,4]{1,0:T(8,128)S(1)} %get-tuple-element.62.flags), custom_call_target="tpu_custom_call" | custom-call | tf_op jit(solution)/shard_map/cond/branch_3_fun/pallas_call | solution.py:443
  35.8 1.5 %shard_map.38 = bf16[128,1536]{1,0:T(8,128)(2,1)} custom-call(bf16[12,128,128]{2,1,0:T(8,128)(2,1)S(1)} %get-tuple-element.82.o, s32[12,4]{1,0:T(8,128)S(1)} %get-tuple-element.81.flags), custom_call_target="tpu_custom_call" | custom-call | tf_op jit(solution)/shard_map/pallas_call | solution.py:495

commit v2 on v1

--- a/solution.py
+++ b/solution.py
@@ -26,16 +26,16 @@
 
 
 PLANS = (
-    (4, 2, 10),
-    (4, 0, 8),
-    (5, 2, 10),
-    (6, 2, 10),
-    (5, 0, 10),
-    (7, 2, 12),
-    (8, 2, 12),
-    (7, 0, 12),
-    (9, 2, 12),
-    (12, 0, 12),
+    (4, 5, 2),
+    (5, 6, 3),
+    (5, 7, 2),
+    (6, 7, 4),
+    (6, 8, 3),
+    (7, 8, 5),
+    (7, 9, 4),
+    (8, 9, 6),
+    (9, 10, 7),
+    (12, 12, 12),
 )
 
 
@@ -43,27 +43,36 @@
     wf = [win[0, h] for h in range(HEADS)]
     wh = [win[1, h] for h in range(HEADS)]
     kinds = [(a - a * b, a * b, b - a * b, (1 - a) * (1 - b)) for a, b in zip(wf, wh)]
-    count = [sum(kind[i] for kind in kinds) for i in range(4)]
-    free = [jnp.int32(0), count[0], count[0] + count[1], count[0] + count[1] + count[2]]
+    lone, two, tall, _ = [sum(kind[i] for kind in kinds) for i in range(4)]
+    best, start, end = jnp.int32(len(PLANS) - 1), jnp.int32(0), jnp.int32(HEADS)
+    for i in reversed(range(len(PLANS) - 1)):
+        nf, nh, both = PLANS[i]
+        fits = (lone + two <= nf) & (two + tall <= nh) & (two <= both)
+        fits = fits & (lone + two + tall <= nf + nh - both)
+        best = jnp.where(fits, i, best)
+        start = jnp.where(fits, nf - both, start)
+        end = jnp.where(fits, nf - both + nh, end)
+    choice[0] = best
+    middle = jnp.maximum(start, lone)
+    gap = middle - lone
+    after = end - tall - middle - two
+    free = [jnp.int32(0), middle, end - 1, jnp.int32(0)]
     ranks = []
     for kind in kinds:
-        ranks.append(sum(x * place for x, place in zip(kind, free)))
-        free = [place + x for x, place in zip(kind, free)]
+        i = free[3]
+        rest = jnp.where(i < gap, lone + i, jnp.where(i < gap + after, middle + two - gap + i, end - gap - after + i))
+        ranks.append(kind[0] * free[0] + kind[1] * free[1] + kind[2] * free[2] + kind[3] * rest)
+        free = [free[0] + kind[0], free[1] + kind[1], free[2] - kind[2], free[3] + kind[3]]
     heads = [sum(jnp.where(ranks[h] == s, h, 0) for h in range(HEADS)) for s in range(HEADS)]
-    wide, lone, tall = count[0] + count[1], count[0], count[1] + count[2]
-    best = jnp.int32(len(PLANS) - 1)
-    for i in reversed(range(len(PLANS) - 1)):
-        nf, h0, h1 = PLANS[i]
-        best = jnp.where((wide <= nf) & (lone >= h0) & (lone + tall <= h1), i, best)
-    choice[0] = best
     for s in range(HEADS):
         for i in range(3):
             flags[s, i] = win[i, heads[s]]
-        flags[s, 3] = ranks[s]
+        flags[s, 3] = ranks[s] % 2 * HALF + ranks[s] // 2
         columns = pl.ds(pl.multiple_of(heads[s] * HD, HD), HD)
-        packed[s % 2, s // 2, 0] = kv[0, :, columns]
-        packed[s % 2, s // 2, 1] = kv[1, :, columns].T
-        packed[s % 2, s // 2, 2] = q[:, columns]
+        at = s % 2 * HALF + s // 2
+        packed[0, at] = kv[0, :, columns]
+        packed[1, at] = kv[1, :, columns].T
+        packed[2, at] = q[:, columns]
 
 
 def place_kernel(o, flags, out):
@@ -98,8 +107,13 @@
     o_s,
     o_r,
 ):
-    nf, h0, h1 = cfg
-    lo, hi = h0 // 2, h1 // 2
+    nf, nh, both = cfg
+    h0 = nf - both
+    h1 = h0 + nh
+
+    def part(start, end, g):
+        return (start + 1 - g) // 2, (end + 1 - g) // 2
+
     f = lax.axis_index("frame")
     height = lax.axis_index("height")
     y = height // 2
@@ -136,8 +150,10 @@
                 )
 
     own_loads = (
-        pltpu.make_async_copy(packed.at[c, :, pl.ds(0, 2)], kv.at[1, :, c], own_l.at[0]),
-        pltpu.make_async_copy(packed.at[c, :, 2], qa.at[:, 0, c], own_l.at[1]),
+        pltpu.make_async_copy(
+            packed.at[pl.ds(0, 2), pl.ds(c * HALF, HALF)], kv.at[1, :, :, c], own_l.at[0]
+        ),
+        pltpu.make_async_copy(packed.at[2, pl.ds(c * HALF, HALF)], qa.at[:, 0, c], own_l.at[1]),
     )
 
     def remote(src, dst, send_sem, recv_sem, device):
@@ -152,36 +168,63 @@
 
     own_copies = (
         remote(
-            packed.at[other, :, pl.ds(0, 2)], kv.at[1, :, c], own_s.at[0], own_r.at[0], partner
+            packed.at[pl.ds(0, 2), pl.ds(other * HALF, HALF)],
+            kv.at[1, :, :, c],
+            own_s.at[0],
+            own_r.at[0],
+            partner,
         ),
-        remote(packed.at[other, :, 2], qa.at[:, 0, c], own_s.at[1], own_r.at[1], partner),
+        remote(
+            packed.at[2, pl.ds(other * HALF, HALF)],
+            qa.at[:, 0, c],
+            own_s.at[1],
+            own_r.at[1],
+            partner,
+        ),
     )
 
-    def z_copy(d, j, g):
+    def z_copy(d, s):
+        j, g = s // 2, s % 2
         return remote(
-            packed.at[g, j, pl.ds(0, 2)],
-            kv.at[2 - 2 * d, j, c],
-            z_s.at[d, j, g],
-            z_r.at[1 - d, j, c],
+            packed.at[pl.ds(0, 2), g * HALF + j],
+            kv.at[2 - 2 * d, :, j, c],
+            z_s.at[d],
+            z_r.at[1 - d, j],
             {"frame": z_dev[d], "height": 2 * y + g},
         )
 
-    def z_arrival(d, j, half):
-        dst = kv.at[2 * d, j, half]
-        return remote(dst, dst, z_s.at[d, j, 0], z_r.at[d, j, half], partner)
-
-    def q_copy(d, j, g):
+    def z_arrival(d, j):
+        dst = kv.at[2 * d, :, j]
+        return remote(dst, dst, z_s.at[d], z_r.at[d, j], partner)
+
+    def z_sent(d):
+        src = packed.at[pl.ds(0, 2), pl.ds(0, nf)]
+        return remote(src, src, z_s.at[d], z_r.at[d, 0], partner)
+
+    runs = ((nf, h1), (h0, nf))
+
+    def q_copy(d, i, g):
+        j, end = part(*runs[i], g)
         return remote(
-            packed.at[g, j, 2],
-            qa.at[j, 2 - d, c],
-            q_s.at[d, j, g],
-            q_r.at[1 - d, j, c],
+            packed.at[2, pl.ds(g * HALF + j, end - j)],
+            qa.at[pl.ds(j, end - j), 2 - d, c],
+            q_s.at[d],
+            q_r.at[1 - d, i],
             {"height": 2 * y_dev[d] + g},
         )
 
-    def q_arrival(d, j, half):
-        dst = qa.at[j, 1 + d, half]
-        return remote(dst, dst, q_s.at[d, j, 0], q_r.at[d, j, half], partner)
+    def q_arrival(d, i, g):
+        j, end = part(*runs[i], g)
+        dst = qa.at[pl.ds(j, end - j), 1 + d]
+        return remote(dst, dst, q_s.at[d], q_r.at[d, i], partner)
+
+    def q_sent(d):
+        src = packed.at[2, pl.ds(0, nh)]
+        return remote(src, src, q_s.at[d], q_r.at[d, 0], partner)
+
+    def filled(i, g):
+        j, end = part(*runs[i], g)
+        return j < end
 
     def ret_copy(d, j):
         return remote(
@@ -193,14 +236,16 @@
         )
 
     def o_copy(j):
-        return remote(oh.at[j, other], out.at[2 * j + c], o_s.at[j], o_r.at[j], partner)
-
-    def o_arrival(j):
-        dst = out.at[2 * j + other]
-        return remote(dst, dst, o_s.at[j], o_r.at[j], partner)
+        return remote(oh.at[other, j], out.at[c * HALF + j], o_s, o_r, partner)
+
+    def o_arrivals():
+        return remote(oh.at[other], out.at[pl.ds(other * HALF, HALF)], o_s, o_r, partner)
 
     def o_store(j):
-        return pltpu.make_async_copy(oh.at[j, c], out.at[2 * j + c], o_l.at[j])
+        return pltpu.make_async_copy(oh.at[c, j], out.at[c * HALF + j], o_l)
+
+    def o_stores():
+        return pltpu.make_async_copy(oh.at[c], out.at[pl.ds(c * HALF, HALF)], o_l)
 
     for copy in own_loads:
         copy.start()
@@ -228,23 +273,20 @@
             @pl.when(z_ok[d])
             def _():
                 for s in slots:
-                    z_copy(d, s // 2, s % 2).start()
+                    z_copy(d, s).start()
 
     z_order = tuple(reversed(range(nf)))
     for copy in own_copies:
         copy.start()
     send_z(z_order[:4])
-    few, most = nf // 2, (nf + 1) // 2
-
-    @pl.loop(lo, hi)
-    def _(n):
-        j = jnp.where(n < most, most - 1 - n + lo, n)
+    for i in range(2):
         for d in range(2):
 
             @pl.when(y_ok[d])
             def _():
                 for g in range(2):
-                    q_copy(d, j, g).start()
+                    if filled(i, g):
+                        q_copy(d, i, g).start()
 
     key_side = lax.broadcasted_iota(jnp.int32, (W, 3 * CHIP), 0) // TW
     query_side = lax.broadcasted_iota(jnp.int32, (W, 3 * CHIP), 1) % W // TW
@@ -255,10 +297,10 @@
         return (1 - flags[2 * j + c, column]).astype(jnp.float32)
 
     def keys(tile, j):
-        return kv[tile, j, :, 0].reshape(CHIP, HD)
+        return kv[tile, 0, j].reshape(CHIP, HD)
 
     def values(tile, j):
-        vt = jnp.concatenate([kv[tile, j, 0, 1], kv[tile, j, 1, 1]], axis=1)
+        vt = jnp.concatenate([kv[tile, 1, j, 0], kv[tile, 1, j, 1]], axis=1)
         return jnp.concatenate([vt, ones], axis=0)
 
     def scores(k, j, parts):
@@ -282,8 +324,7 @@
 
             @pl.when(z_ok[d])
             def _():
-                for half in range(2):
-                    z_arrival(d, j, half).wait_recv()
+                z_arrival(d, j).wait_recv()
 
         n = parts * CHIP
         s = scores(jnp.concatenate([keys(0, j), keys(2, j)], axis=0), j, parts)
@@ -320,8 +361,8 @@
 
     def finish(j, o):
         o = o.T.astype(jnp.bfloat16)
-        oh[j, 0] = o[:TOK]
-        oh[j, 1] = o[TOK:]
+        oh[0, j] = o[:TOK]
+        oh[1, j] = o[TOK:]
         o_copy(j).start()
         o_store(j).start()
 
@@ -334,6 +375,7 @@
             @pl.when(y_ok[d])
             def _():
                 ret_copy(1 - d, j).wait_recv()
+                ret_copy(d, j).wait_send()
 
         m = top[j, 0:1, 0:CHIP] * SCALE
         total = acc[j, HD : HD + 1, 0:CHIP]
@@ -356,88 +398,77 @@
     for copy in own_copies:
         copy.wait_recv()
 
-    if lo + HALF - hi > 0:
-
-        @pl.loop(0, lo + HALF - hi)
-        def _(n):
-            j = jnp.where(n < lo, n, n - lo + hi)
-            here(j, 1)
-
-            @pl.when(j >= hi)
-            def _():
-                alone(j)
-
-    send_z(z_order[4:])
-
-    my_z = (nf + 1 - c) // 2
+    lo, hi = part(h0, h1, c)
+    my_z = part(0, nf, c)[1]
     n_in = my_z - lo
     n_out = hi - my_z
 
-    @pl.loop(0, 2 * n_in + n_out)
+    @pl.loop(0, lo + HALF - hi)
     def _(n):
-        outer = (n == n_in) | (n > n_in + n_out)
-        j_in = jnp.where(n < n_in, my_z - 1 - n, my_z - 1 + n - n_in)
-        j_out = jnp.where(n == n_in, my_z - 1, my_z - 1 - (n - n_in - n_out))
-        j = jnp.where(outer, j_out, j_in)
+        j = jnp.where(n < lo, n, n - lo + hi)
+        here(j, 1)
+
+        @pl.when(j >= hi)
+        def _():
+            alone(j)
+
+    send_z(z_order[4:])
+
+    @pl.loop(0, n_out + 2 * n_in)
+    def _(n):
+        outer = n >= n_out + n_in
+        j = jnp.where(n < n_out, my_z + n, my_z - 1 - (n - n_out) + jnp.where(outer, n_in, 0))
+        for i in range(2):
+            for d in range(2):
+                for g in range(2):
+                    if filled(i, g):
+
+                        @pl.when((n == (n_out if i else 0)) & (c == g) & y_ok[d])
+                        def _():
+                            q_arrival(d, i, g).wait_recv()
 
         @pl.when(jnp.logical_not(outer))
         def _():
-            for d in range(2):
-
-                @pl.when(y_ok[d])
-                def _():
-                    for half in range(2):
-                        q_arrival(d, j, half).wait_recv()
-
             here(j, 3)
 
         @pl.when(outer)
         def _():
             around(j, 3)
 
-        @pl.when(n >= n_in)
+        @pl.when(outer | (n < n_out))
         def _():
             give_back(j)
 
-    for copy in own_copies:
-        copy.wait_send()
-
-    if lo > 0:
+    if h0 > 0:
 
         @pl.loop(0, lo)
         def _(j):
             around(j, 1)
             alone(j)
 
+    for copy in own_copies:
+        copy.wait_send()
+    for d in range(2):
+
+        @pl.when(z_ok[d])
+        def _():
+            z_sent(d).wait_send()
+
+        @pl.when(y_ok[d])
+        def _():
+            q_sent(d).wait_send()
+
     @pl.loop(0, hi - lo)
     def _(n):
         join(jnp.where(n < n_out, my_z + n, my_z - 1 - (n - n_out)))
 
-    for d in range(2):
-
-        @pl.when(z_ok[d])
-        def _():
-            for s in range(nf):
-                z_copy(d, s // 2, s % 2).wait_send()
-
-        @pl.when(y_ok[d])
-        def _():
-            @pl.loop(lo, hi)
-            def _(j):
-                for g in range(2):
-                    q_copy(d, j, g).wait_send()
-                ret_copy(d, j).wait_send()
-
-    @pl.loop(0, HALF)
-    def _(j):
-        o_store(j).wait()
-        o_copy(j).wait_send()
-        o_arrival(j).wait_recv()
+    o_stores().wait()
+    o_arrivals().wait()
 
 
 def attend(index, n_frame, n_chip_y, packed, flags):
-    nf, h0, h1 = PLANS[index]
-    assert h0 % 2 == 0 and h1 % 2 == 0 and h0 < nf - 1 and nf <= h1
+    nf, nh, both = PLANS[index]
+    assert both <= min(nf, nh) and nf + nh - both <= HEADS
     bf16, f32 = jnp.bfloat16, jnp.float32
     dma = pltpu.SemaphoreType.DMA
     return pl.pallas_call(
@@ -446,25 +477,25 @@
         in_specs=[pl.BlockSpec(memory_space=pl.ANY), pl.BlockSpec(memory_space=pltpu.SMEM)],
         out_specs=pl.BlockSpec(memory_space=pl.ANY),
         scratch_shapes=[
-            pltpu.VMEM((3, HALF, 2, 2, TOK, HD), bf16),
+            pltpu.VMEM((3, 2, HALF, 2, TOK, HD), bf16),
             pltpu.VMEM((HALF, 3, 2, TOK, HD), bf16),
             pltpu.VMEM((HALF, HD + EXTRA, 3 * CHIP), f32),
             pltpu.VMEM((HALF, 8, 3 * CHIP), f32),
             pltpu.VMEM((2, HALF, HD + EXTRA, CHIP), bf16),
             pltpu.VMEM((2, HALF, HD + EXTRA, CHIP), bf16),
-            pltpu.VMEM((HALF, 2, TOK, HD), bf16),
+            pltpu.VMEM((2, HALF, TOK, HD), bf16),
             dma((2,)),
             dma((2,)),
             dma((2,)),
-            dma((2, HALF, 2)),
-            dma((2, HALF, 2)),
-            dma((2, HALF, 2)),
-            dma((2, HALF, 2)),
+            dma((2,)),
+            dma((2, HALF)),
+            dma((2,)),
+            dma((2, 2)),
             dma((2, HALF)),
             dma((2, HALF)),
-            dma((HALF,)),
-            dma((HALF,)),
-            dma((HALF,)),
+            dma,
+            dma,
+            dma,
         ],
         compiler_params=pltpu.CompilerParams(
             collective_id=index,
@@ -483,7 +514,7 @@
     packed, flags, choice = pl.pallas_call(
         sort_kernel,
         out_shape=(
-            jax.ShapeDtypeStruct((2, HALF, 3, TOK, HD), jnp.bfloat16),
+            jax.ShapeDtypeStruct((3, HEADS, TOK, HD), jnp.bfloat16),
             jax.ShapeDtypeStruct((HEADS, 4), jnp.int32),
             jax.ShapeDtypeStruct((1,), jnp.int32),
         ),

time: 37.4 us -> 33.6 us (0.90)
  Pallas kernels: 36.3 us -> 32.6 us
    pallas_call x1, Pallas kernels: 32.4 us -> 28.6 us  [attend(): pl.pallas_call(functools.partial(kernel, PLANS[index], n_frame, n_chip_y)...]
where the time goes in v2:
time: 33.6 us; the launch traced here: 33.5 us
  Pallas kernels  32.6 us (97%)
  between operations  0.67 us (2%)
    pallas_call x1, Pallas kernels, attend(): pl.pallas_call(functools.partial(kernel, PLANS[index], n_frame, n_chip_y)...  28.6 us
    pallas_call x1, Pallas kernels, shards(): pl.pallas_call(sort_kernel, out_shape=(jax.ShapeDtypeStruct((3, HEADS, TO...  2.53 us
    pallas_call x1, Pallas kernels, shards(): pl.pallas_call(place_kernel, out_shape=jax.ShapeDtypeStruct((TOK, width),...  1.49 us

profile of v2, /device:TPU:31, one launch (start us, length us, event | category | flops | bytes accessed | tf_op | source)
XLA Modules:
  0.0 33.5 jit_solution(10543736254871922600)
XLA Ops:
  0.0 2.5 %shard_map.37 = (bf16[3,12,128,128]{3,2,1,0:T(8,128)(2,1)S(1)}, s32[12,4]{1,0:T(8,128)S(1)}, s32[1]{0:T(128)}) custom-call(bf16[128,1536]{1,0:T(8,128)(2,1)} %bitcast.6, bf16[2,128,1536]{2,1,0:T(8,128)(2,1)} %bitcast.5, s32[3,12]{1,0:T(4,128)} %bitcast.7), custom_call_target="tpu_custom_call" | custom-call | tf_op jit(solution)/shard_map/pallas_call | solution.py:514
  3.2 28.8 %conditional.1 = (bf16[12,128,128]{2,1,0:T(8,128)(2,1)S(1)}) conditional(s32[]{:T(128)} %bitcast.3, (bf16[3,12,128,128]{3,2,1,0:T(8,128)(2,1)S(1)}, s32[12,4]{1,0:T(8,128)S(1)}) %tuple.35, (bf16[3,12,128,128]{3,2,1,0:T(8,128)(2,1)S(1)}, s32[12,4]{1,0:T(8,128)S(1)}) %tuple.35, ...), branch_computations={%region_0.0_spmd, %region_1.0_spmd, %region_2.0_spmd, %region_3.0_... | conditional | bytes 8 | solution.py:525
  3.2 28.6 %branch_1_fun.1 = bf16[12,128,128]{2,1,0:T(8,128)(2,1)S(1)} custom-call(bf16[3,12,128,128]{3,2,1,0:T(8,128)(2,1)S(1)} %get-tuple-element.50.packed, s32[12,4]{1,0:T(8,128)S(1)} %get-tuple-element.54.flags), custom_call_target="tpu_custom_call" | custom-call | tf_op jit(solution)/shard_map/cond/branch_1_fun/pallas_call | solution.py:474
  32.0 1.5 %shard_map.38 = bf16[128,1536]{1,0:T(8,128)(2,1)} custom-call(bf16[12,128,128]{2,1,0:T(8,128)(2,1)S(1)} %get-tuple-element.82.o, s32[12,4]{1,0:T(8,128)S(1)} %get-tuple-element.81.flags), custom_call_target="tpu_custom_call" | custom-call | tf_op jit(solution)/shard_map/pallas_call | solution.py:526
